TPU v7x, 32 devices: a whole 2x2x4 slice. The times are simulated.
32 devices in a mesh: seq: 8 (over z, y), mp: 4 (over x, core).
Axes of the slice: x: 2, y: 2, z: 4, core: 2. Of those that a mesh axis runs over, the one named last changes fastest.
Arguments:
- queries: bfloat16 [3072, 2048], P('seq', 'mp'), may hold values from -110 to 110
- self_keys: bfloat16 [3072, 2048], P('seq', 'mp'), may hold values from -6 to 6
- self_values: bfloat16 [3072, 2048], P('seq', 'mp'), may hold values from -6 to 6
- cross_query: bfloat16 [3072, 2048], P('seq', 'mp'), may hold values from -110 to 110
- memory_keys: bfloat16 [64, 128, 2048], P('seq', None, 'mp'), may hold values from -6 to 6
- memory_values: bfloat16 [64, 128, 2048], P('seq', None, 'mp'), may hold values from -6 to 6
- neighbour_owner: int32 [48, 2], P('seq'), may hold values from 0 to 7, all different within a row; in each aligned block of 6 rows (0 to 5, 6 to 11, ...) at most 2 rows name the same one
- neighbour_slot: int32 [48, 2], P('seq'), may hold values from 0 to 7
- out_weight: bfloat16 [2048, 4096], P('mp'), may hold values from -0.125 to 0.125
- cross_weight: bfloat16 [2048, 4096], P('mp'), may hold values from -0.125 to 0.125
Outputs:
- block_out: bfloat16 [3072, 4096], P('seq', 'mp')
Inputs may be any that keep to these rules, and one draw needn't show every extreme that they name: `neighbour_owner`: the 2 neighbours of a span have different owners; among the spans of one index of seq, at most 2 neighbours have one owner.
All inputs are finite; a program needn't handle non-finite values.
Results may differ from a plain program's by a relative error of at most 0.025.
Values may be sent and summed in bfloat16 or wider, within the bound.
A program may use at most 128 MiB of HBM per device.

v0:
```python
import jax
import jax.numpy as jnp
from jax import lax
from jax.sharding import PartitionSpec as P

HEAD = 128
SPAN = 64
NEG_FILL = -1e30


def from_behind(value, axis, steps):
    count = lax.axis_size(axis)
    leading, last = (max(0, -steps), min(count, count - steps))
    return lax.ppermute(value, axis, [(source, source + steps) for source in range(leading, last)])


def split_heads(matrix_block, head_width):
    return matrix_block.reshape(
        matrix_block.shape[:-1] + (matrix_block.shape[-1] // head_width, head_width)
    )


def attend_block(carried, queries, key_value, causal):
    running, totals, numerator = carried
    query_heads = split_heads(queries, HEAD)
    key_heads = split_heads(key_value[0], HEAD)
    value_heads = split_heads(key_value[1], HEAD)
    scores = jnp.einsum(
        "tha,uha->htu", query_heads, key_heads, preferred_element_type=jnp.float32
    ) * HEAD ** (-0.5)
    row_count = queries.shape[0]
    causal_ok = lax.broadcasted_iota(jnp.int32, (row_count, row_count), 0) >= lax.broadcasted_iota(
        jnp.int32, (row_count, row_count), 1
    )
    allowed = jnp.logical_or(causal_ok, jnp.logical_not(causal))
    masked = jnp.where(allowed[None], scores, NEG_FILL)
    newest = jnp.maximum(running, jnp.max(masked, axis=2))
    weights = jnp.exp(masked - newest[..., None])
    factor = jnp.exp(running - newest)
    totals = totals * factor + jnp.sum(weights, axis=2)
    numerator = numerator * factor[..., None] + jnp.einsum(
        "htu,uha->hta",
        weights.astype(jnp.bfloat16),
        value_heads,
        preferred_element_type=jnp.float32,
    )
    return (newest, totals, numerator)


def visit(carried, queries, key_value, source, own_index):
    return lax.cond(
        source < own_index,
        lambda status: attend_block(status, queries, key_value, False),
        lambda status: status,
        carried,
    )


def pass_lower(key_value):
    return from_behind(key_value, "seq", 1)


def self_attention(queries, self_keys, self_values):
    devices = lax.axis_size("seq")
    own_index = lax.axis_index("seq")
    row_count = queries.shape[0]
    heads_here = queries.shape[1] // HEAD
    key_value = jnp.stack([self_keys, self_values])
    initial = (
        jnp.full((heads_here, row_count), NEG_FILL, jnp.float32),
        jnp.zeros((heads_here, row_count), jnp.float32),
        jnp.zeros((heads_here, row_count, HEAD), jnp.float32),
    )
    carried = attend_block(initial, queries, key_value, True)

    def one_way(turn_index, status):
        travel, inner_state = status
        travel = pass_lower(travel)
        return (
            travel,
            visit(inner_state, queries, travel, (own_index - turn_index) % devices, own_index),
        )

    travel, carried = lax.fori_loop(1, devices, one_way, (key_value, carried))
    running, totals, numerator = carried
    blended = numerator / totals[..., None]
    return (
        jnp.transpose(blended, (1, 0, 2)).reshape(row_count, heads_here * HEAD).astype(jnp.bfloat16)
    )


def cross_attention(cross_query, memory_keys, memory_values, neighbour_owner, neighbour_slot):
    devices = lax.axis_size("seq")
    span_count = neighbour_owner.shape[0]
    pick_count = neighbour_owner.shape[1]
    request_count = span_count * pick_count
    capacity = max(2, (request_count + devices - 1) // devices)
    slot_total = devices * capacity
    feature_count = cross_query.shape[1]
    heads_here = feature_count // HEAD
    owner_list = neighbour_owner.reshape(request_count)
    slot_list = neighbour_slot.reshape(request_count)
    owner_hits = (owner_list[:, None] == jnp.arange(devices, dtype=jnp.int32)[None, :]).astype(
        jnp.int32
    )
    earlier = jnp.cumsum(owner_hits, axis=0) - owner_hits
    rank_within = jnp.sum(earlier * owner_hits, axis=1)
    target_slot = owner_list * capacity + rank_within
    routing = target_slot[:, None] == jnp.arange(slot_total, dtype=jnp.int32)[None, :]
    span_rows = cross_query.reshape(span_count, SPAN * feature_count)
    request_rows = jnp.repeat(span_rows, pick_count, axis=0)
    outgoing = jnp.dot(
        jnp.transpose(routing).astype(jnp.bfloat16),
        request_rows,
        preferred_element_type=jnp.float32,
    ).astype(jnp.bfloat16)
    outgoing = outgoing.reshape(devices, capacity, SPAN, feature_count)
    asked_slots = jnp.sum(jnp.where(routing, slot_list[:, None], 0), axis=0).reshape(
        devices, capacity
    )
    asked = lax.all_to_all(outgoing, "seq", split_axis=0, concat_axis=0, tiled=True)
    wanted = lax.all_to_all(asked_slots, "seq", split_axis=0, concat_axis=0, tiled=True)
    source_count = wanted.shape[0]
    item_count = wanted.shape[1]
    key_heads = split_heads(memory_keys[wanted], HEAD)
    value_heads = split_heads(memory_values[wanted], HEAD)
    query_heads = split_heads(asked, HEAD)
    scores = jnp.einsum(
        "nicha,nikha->nihck", query_heads, key_heads, preferred_element_type=jnp.float32
    ) * HEAD ** (-0.5)
    highest = jnp.max(scores, axis=4)
    weights = jnp.exp(scores - highest[..., None])
    totals = jnp.sum(weights, axis=4)
    blended = jnp.einsum(
        "nihck,nikha->nicha",
        weights.astype(jnp.bfloat16),
        value_heads,
        preferred_element_type=jnp.float32,
    )
    blended = blended / jnp.transpose(totals, (0, 1, 3, 2))[..., None]
    answer = blended.reshape(source_count, item_count, SPAN, feature_count).astype(jnp.bfloat16)
    log_mass = highest + jnp.log(totals)
    answers = lax.all_to_all(answer, "seq", split_axis=0, concat_axis=0, tiled=True)
    log_masses = lax.all_to_all(
        log_mass.astype(jnp.bfloat16), "seq", split_axis=0, concat_axis=0, tiled=True
    ).astype(log_mass.dtype)
    answer_rows = jnp.dot(
        routing.astype(jnp.bfloat16),
        answers.reshape(slot_total, SPAN * feature_count),
        preferred_element_type=jnp.float32,
    )
    mass_rows = jnp.dot(
        routing.astype(jnp.float32),
        log_masses.reshape(slot_total, heads_here * SPAN),
        precision=lax.Precision.HIGHEST,
    )
    answer_rows = answer_rows.reshape(span_count, pick_count, SPAN, heads_here, HEAD)
    mass_rows = mass_rows.reshape(span_count, pick_count, heads_here, SPAN)
    best_mass = jnp.max(mass_rows, axis=1, keepdims=True)
    shares = jnp.exp(mass_rows - best_mass)
    share_cols = jnp.transpose(shares, (0, 1, 3, 2))[..., None]
    combined = jnp.sum(share_cols * answer_rows, axis=1) / jnp.sum(share_cols, axis=1)
    return combined.reshape(span_count * SPAN, feature_count).astype(jnp.bfloat16)


def per_device(
    queries,
    self_keys,
    self_values,
    cross_query,
    memory_keys,
    memory_values,
    neighbour_owner,
    neighbour_slot,
    out_weight,
    cross_weight,
):
    attended = self_attention(queries, self_keys, self_values)
    retrieved = cross_attention(
        cross_query, memory_keys, memory_values, neighbour_owner, neighbour_slot
    )
    partial_value = jnp.dot(attended, out_weight, preferred_element_type=jnp.float32)
    partial_value = partial_value + jnp.dot(
        retrieved, cross_weight, preferred_element_type=jnp.float32
    )
    return lax.psum_scatter(
        partial_value.astype(jnp.bfloat16), "mp", scatter_dimension=1, tiled=True
    )


def solution(mesh):
    placed = (
        P("seq", "mp"),
        P("seq", "mp"),
        P("seq", "mp"),
        P("seq", "mp"),
        P("seq", None, "mp"),
        P("seq", None, "mp"),
        P("seq", None),
        P("seq", None),
        P("mp", None),
        P("mp", None),
    )
    return jax.shard_map(
        per_device, mesh=mesh, in_specs=placed, out_specs=P("seq", "mp"), check_vma=False
    )
```

profile of v0, /device:TPU:0, one launch (start us, length us, event | category | flops | bytes accessed | tf_op | source)
XLA Modules:
  0.0 320.3 jit_solution(1754445644933671382)
XLA Ops:
  9.3 7.3 %all-to-all-start.1 = ((s32[8,1,2]{2,1,0:T(1,128)}), s32[8,1,2]{2,1,0:T(1,128)S(1)}, u32[]{:S(2)}, u32[]{:S(2)}) async-start(s32[8,1,2]{2,1,0:T(1,128)} %bitcast.9), calls=%async_computation.1 | async-start | bytes 8192 | tf_op jit(solution)/shard_map/all_to_all | solution.py:122
  23.0 4.2 %all-to-all-start = ((bf16[8,2,64,512]{3,2,1,0:T(8,128)(2,1)}), bf16[8,2,64,512]{3,2,1,0:T(8,128)(2,1)}, u32[]{:S(2)}, u32[]{:S(2)}) async-start(bf16[8,2,64,512]{3,2,1,0:T(8,128)(2,1)} %bitcast.39), calls=%async_computation | async-start | bytes 2097152 | tf_op jit(solution)/shard_map/all_to_all | solution.py:121
  40.0 12.4 %all-to-all-done = bf16[8,2,64,512]{3,2,1,0:T(8,128)(2,1)} async-done(((bf16[8,2,64,512]{3,2,1,0:T(8,128)(2,1)}), bf16[8,2,64,512]{3,2,1,0:T(8,128)(2,1)}, u32[]{:S(2)}, u32[]{:S(2)}) %all-to-all-start) | async-done | bytes 1048608 | tf_op jit(solution)/shard_map/all_to_all | solution.py:121
  52.4 3.6 %multiply_reduce_fusion.2 = (f32[8,2,4,64]{3,2,1,0:T(4,128)S(1)}, f32[8,2,4,64,128]{4,3,2,1,0:T(8,128)S(1)}) fusion(bf16[8,2,128,4,128]{4,3,2,1,0:T(4,128)(2,1)} %reshape.152, bf16[8,2,64,512]{3,2,1,0:T(8,128)(2,1)} %all-to-all-done), kind=kOutput, calls=%fused_computation.28 | convolution fusion | flops 135262208 | bytes 5259264 | tf_op jit(solution)/shard_map/nicha,nikha->nihck/dot_general | solution.py:128
  60.0 3.4 %all-to-all-start.2 = ((bf16[8,2,256]{2,1,0:T(2,128)(2,1)}), bf16[8,2,256]{2,1,0:T(2,128)(2,1)S(1)}, u32[]{:S(2)}, u32[]{:S(2)}) async-start(bf16[8,2,256]{2,1,0:T(2,128)(2,1)} %reshape.180), calls=%async_computation.2 | async-start | bytes 16384 | tf_op jit(solution)/shard_map/all_to_all | solution.py:144
  69.8 4.3 %all-to-all-start.3 = ((bf16[8,2,64,512]{3,2,1,0:T(8,128)(2,1)}), bf16[8,2,64,512]{3,2,1,0:T(8,128)(2,1)}, u32[]{:S(2)}, u32[]{:S(2)}) async-start(bf16[8,2,64,512]{3,2,1,0:T(8,128)(2,1)} %bitcast.118), calls=%async_computation.3 | async-start | bytes 2097152 | tf_op jit(solution)/shard_map/all_to_all | solution.py:143
  77.9 163.0 %while.21 = (s32[]{:T(128)}, bf16[2,384,512]{1,2,0:T(8,128)(2,1)}, f32[4,384]{1,0:T(4,128)S(1)}, f32[4,384]{1,0:T(4,128)S(1)}, f32[4,384,128]{2,1,0:T(8,128)S(1)...) while((s32[]{:T(128)}, bf16[2,384,512]{1,2,0:T(8,128)(2,1)}, ...), condition=%wide.region_7.8_spmd, body=%wide.region_2.7_spmd.sunk | while | flops 307104768 | bytes 16220540 | solution.py:84
  77.9 3.6 %collective-permute-start = (bf16[2,384,512]{1,2,0:T(8,128)(2,1)}, bf16[2,384,512]{1,2,0:T(8,128)(2,1)S(1)}, u32[]{:S(2)}, u32[]{:S(2)}) collective-permute-start(bf16[2,384,512]{1,2,0:T(8,128)(2,1)} %get-tuple-element.321), channel_id=1, source_target_pairs={{0,4},{4,8},{8,12},{12,16},{16,20},{20,24},{24,28},{1,5},{5,9},{9,... | collective-permute-start | bytes 2359304 | tf_op jit(solution)/shard_map/while/body/eval_jaxpr/ppermute | solution.py:14
  81.6 19.9 %collective-permute-done = bf16[2,384,512]{1,2,0:T(8,128)(2,1)S(1)} collective-permute-done((bf16[2,384,512]{1,2,0:T(8,128)(2,1)}, bf16[2,384,512]{1,2,0:T(8,128)(2,1)S(1)}, u32[]{:S(2)}, u32[]{:S(2)}) %collective-permute-start) | collective-permute-done | bytes 786464 | tf_op jit(solution)/shard_map/while/body/eval_jaxpr/ppermute | solution.py:14
  102.3 12.8 %collective-permute-start = (bf16[2,384,512]{1,2,0:T(8,128)(2,1)}, bf16[2,384,512]{1,2,0:T(8,128)(2,1)S(1)}, u32[]{:S(2)}, u32[]{:S(2)}) collective-permute-start(bf16[2,384,512]{1,2,0:T(8,128)(2,1)} %get-tuple-element.321), channel_id=1, source_target_pairs={{0,4},{4,8},{8,12},{12,16},{16,20},{20,24},{24,28},{1,5},{5,9},{9,... | collective-permute-start | bytes 2359304 | tf_op jit(solution)/shard_map/while/body/eval_jaxpr/ppermute | solution.py:14
  115.2 14.9 %collective-permute-done = bf16[2,384,512]{1,2,0:T(8,128)(2,1)S(1)} collective-permute-done((bf16[2,384,512]{1,2,0:T(8,128)(2,1)}, bf16[2,384,512]{1,2,0:T(8,128)(2,1)S(1)}, u32[]{:S(2)}, u32[]{:S(2)}) %collective-permute-start) | collective-permute-done | bytes 786464 | tf_op jit(solution)/shard_map/while/body/eval_jaxpr/ppermute | solution.py:14
  131.0 5.2 %collective-permute-start = (bf16[2,384,512]{1,2,0:T(8,128)(2,1)}, bf16[2,384,512]{1,2,0:T(8,128)(2,1)S(1)}, u32[]{:S(2)}, u32[]{:S(2)}) collective-permute-start(bf16[2,384,512]{1,2,0:T(8,128)(2,1)} %get-tuple-element.321), channel_id=1, source_target_pairs={{0,4},{4,8},{8,12},{12,16},{16,20},{20,24},{24,28},{1,5},{5,9},{9,... | collective-permute-start | bytes 2359304 | tf_op jit(solution)/shard_map/while/body/eval_jaxpr/ppermute | solution.py:14
  136.3 14.0 %collective-permute-done = bf16[2,384,512]{1,2,0:T(8,128)(2,1)S(1)} collective-permute-done((bf16[2,384,512]{1,2,0:T(8,128)(2,1)}, bf16[2,384,512]{1,2,0:T(8,128)(2,1)S(1)}, u32[]{:S(2)}, u32[]{:S(2)}) %collective-permute-start) | collective-permute-done | bytes 786464 | tf_op jit(solution)/shard_map/while/body/eval_jaxpr/ppermute | solution.py:14
  151.1 12.3 %collective-permute-start = (bf16[2,384,512]{1,2,0:T(8,128)(2,1)}, bf16[2,384,512]{1,2,0:T(8,128)(2,1)S(1)}, u32[]{:S(2)}, u32[]{:S(2)}) collective-permute-start(bf16[2,384,512]{1,2,0:T(8,128)(2,1)} %get-tuple-element.321), channel_id=1, source_target_pairs={{0,4},{4,8},{8,12},{12,16},{16,20},{20,24},{24,28},{1,5},{5,9},{9,... | collective-permute-start | bytes 2359304 | tf_op jit(solution)/shard_map/while/body/eval_jaxpr/ppermute | solution.py:14
  163.5 15.4 %collective-permute-done = bf16[2,384,512]{1,2,0:T(8,128)(2,1)S(1)} collective-permute-done((bf16[2,384,512]{1,2,0:T(8,128)(2,1)}, bf16[2,384,512]{1,2,0:T(8,128)(2,1)S(1)}, u32[]{:S(2)}, u32[]{:S(2)}) %collective-permute-start) | collective-permute-done | bytes 786464 | tf_op jit(solution)/shard_map/while/body/eval_jaxpr/ppermute | solution.py:14
  179.8 5.2 %collective-permute-start = (bf16[2,384,512]{1,2,0:T(8,128)(2,1)}, bf16[2,384,512]{1,2,0:T(8,128)(2,1)S(1)}, u32[]{:S(2)}, u32[]{:S(2)}) collective-permute-start(bf16[2,384,512]{1,2,0:T(8,128)(2,1)} %get-tuple-element.321), channel_id=1, source_target_pairs={{0,4},{4,8},{8,12},{12,16},{16,20},{20,24},{24,28},{1,5},{5,9},{9,... | collective-permute-start | bytes 2359304 | tf_op jit(solution)/shard_map/while/body/eval_jaxpr/ppermute | solution.py:14
  185.0 14.5 %collective-permute-done = bf16[2,384,512]{1,2,0:T(8,128)(2,1)S(1)} collective-permute-done((bf16[2,384,512]{1,2,0:T(8,128)(2,1)}, bf16[2,384,512]{1,2,0:T(8,128)(2,1)S(1)}, u32[]{:S(2)}, u32[]{:S(2)}) %collective-permute-start) | collective-permute-done | bytes 786464 | tf_op jit(solution)/shard_map/while/body/eval_jaxpr/ppermute | solution.py:14
  200.4 7.2 %collective-permute-start = (bf16[2,384,512]{1,2,0:T(8,128)(2,1)}, bf16[2,384,512]{1,2,0:T(8,128)(2,1)S(1)}, u32[]{:S(2)}, u32[]{:S(2)}) collective-permute-start(bf16[2,384,512]{1,2,0:T(8,128)(2,1)} %get-tuple-element.321), channel_id=1, source_target_pairs={{0,4},{4,8},{8,12},{12,16},{16,20},{20,24},{24,28},{1,5},{5,9},{9,... | collective-permute-start | bytes 2359304 | tf_op jit(solution)/shard_map/while/body/eval_jaxpr/ppermute | solution.py:14
  207.7 13.6 %collective-permute-done = bf16[2,384,512]{1,2,0:T(8,128)(2,1)S(1)} collective-permute-done((bf16[2,384,512]{1,2,0:T(8,128)(2,1)}, bf16[2,384,512]{1,2,0:T(8,128)(2,1)S(1)}, u32[]{:S(2)}, u32[]{:S(2)}) %collective-permute-start) | collective-permute-done | bytes 786464 | tf_op jit(solution)/shard_map/while/body/eval_jaxpr/ppermute | solution.py:14
  222.2 5.2 %collective-permute-start = (bf16[2,384,512]{1,2,0:T(8,128)(2,1)}, bf16[2,384,512]{1,2,0:T(8,128)(2,1)S(1)}, u32[]{:S(2)}, u32[]{:S(2)}) collective-permute-start(bf16[2,384,512]{1,2,0:T(8,128)(2,1)} %get-tuple-element.321), channel_id=1, source_target_pairs={{0,4},{4,8},{8,12},{12,16},{16,20},{20,24},{24,28},{1,5},{5,9},{9,... | collective-permute-start | bytes 2359304 | tf_op jit(solution)/shard_map/while/body/eval_jaxpr/ppermute | solution.py:14
  227.4 12.7 %collective-permute-done = bf16[2,384,512]{1,2,0:T(8,128)(2,1)S(1)} collective-permute-done((bf16[2,384,512]{1,2,0:T(8,128)(2,1)}, bf16[2,384,512]{1,2,0:T(8,128)(2,1)S(1)}, u32[]{:S(2)}, u32[]{:S(2)}) %collective-permute-start) | collective-permute-done | bytes 786464 | tf_op jit(solution)/shard_map/while/body/eval_jaxpr/ppermute | solution.py:14
  241.3 6.7 %fusion.65 = f32[384,4096]{1,0:T(8,128)} fusion(bf16[384,512]{0,1:T(8,128)(2,1)S(1)} %bitcast.128, bf16[512,4096]{1,0:T(8,128)(2,1)} %param.22), kind=kOutput, calls=%fused_computation.89 | convolution fusion | flops 1610612736 | bytes 10878976 | tf_op jit(solution)/shard_map/dot_general | solution.py:182
  258.2 3.6 %add_convert_fusion = bf16[384,4096]{1,0:T(8,128)(2,1)} fusion(f32[384,4096]{1,0:T(8,128)S(1)} %bitcast.122, bf16[512,4096]{1,0:T(8,128)(2,1)S(1)} %copy-done.2, bf16[48,8,4,128]{3,2,1,0:T(4,128)(2,1)S(1)} %bitcast.125), kind=kOutput, calls=%fused_computation.16 | convolution fusion | flops 1613758464 | bytes 14024704 | tf_op jit(solution)/shard_map/dot_general | solution.py:183
  261.8 51.7 %reduce-scatter.2.cloned.1.call-done = bf16[384,1024]{1,0:T(8,128)(2,1)} async-done(((bf16[384,4096]{1,0:T(8,128)(2,1)}), bf16[384,1024]{1,0:T(8,128)(2,1)}) %reduce-scatter.2.cloned.1.call-update) | async-done | bytes 786448 | tf_op jit(solution)/shard_map/reduce_scatter | solution.py:186
  (113 shorter events, 52.6 us)
Async XLA Ops:
  6.5 26.7 %copy-start = (bf16[8,128,512]{2,1,0:T(8,128)(2,1)S(1)}, bf16[8,128,512]{2,1,0:T(8,128)(2,1)}, u32[]{:S(2)}) copy-start(bf16[8,128,512]{2,1,0:T(8,128)(2,1)} %param.19) | copy-start | bytes 3145732
  9.3 13.7 %all-to-all-start.1 = ((s32[8,1,2]{2,1,0:T(1,128)}), s32[8,1,2]{2,1,0:T(1,128)S(1)}, u32[]{:S(2)}, u32[]{:S(2)}) async-start(s32[8,1,2]{2,1,0:T(1,128)} %bitcast.9), calls=%async_computation.1 | async-start | bytes 8192 | tf_op jit(solution)/shard_map/all_to_all | solution.py:122
  19.3 8.6 %copy-start.8 = (bf16[384,512]{1,0:T(8,128)(2,1)S(1)}, bf16[384,512]{1,0:T(8,128)(2,1)}, u32[]{:S(2)}) copy-start(bf16[384,512]{1,0:T(8,128)(2,1)} %param.15) | copy-start | bytes 1179652
  19.4 9.5 %copy-start.9 = (bf16[384,512]{1,0:T(8,128)(2,1)S(1)}, bf16[384,512]{1,0:T(8,128)(2,1)}, u32[]{:S(2)}) copy-start(bf16[384,512]{1,0:T(8,128)(2,1)} %param.16) | copy-start | bytes 1179652
  20.7 9.1 %copy-start.1 = (bf16[384,512]{1,0:T(8,128)(2,1)S(1)}, bf16[384,512]{1,0:T(8,128)(2,1)}, u32[]{:S(2)}) copy-start(bf16[384,512]{1,0:T(8,128)(2,1)} %param.14) | copy-start | bytes 1179652
  23.0 29.4 %all-to-all-start = ((bf16[8,2,64,512]{3,2,1,0:T(8,128)(2,1)}), bf16[8,2,64,512]{3,2,1,0:T(8,128)(2,1)}, u32[]{:S(2)}, u32[]{:S(2)}) async-start(bf16[8,2,64,512]{3,2,1,0:T(8,128)(2,1)} %bitcast.39), calls=%async_computation | async-start | bytes 2097152 | tf_op jit(solution)/shard_map/all_to_all | solution.py:121
  60.0 9.9 %all-to-all-start.2 = ((bf16[8,2,256]{2,1,0:T(2,128)(2,1)}), bf16[8,2,256]{2,1,0:T(2,128)(2,1)S(1)}, u32[]{:S(2)}, u32[]{:S(2)}) async-start(bf16[8,2,256]{2,1,0:T(2,128)(2,1)} %reshape.180), calls=%async_computation.2 | async-start | bytes 16384 | tf_op jit(solution)/shard_map/all_to_all | solution.py:144
  66.0 8.3 %copy-start.4 = (bf16[384,512]{0,1:T(8,128)(2,1)S(1)}, bf16[384,512]{0,1:T(8,128)(2,1)}, u32[]{:S(2)}) copy-start(bf16[384,512]{0,1:T(8,128)(2,1)} %copy.107) | copy-start | bytes 1179652
  66.0 8.3 %copy-start.5 = (bf16[384,512]{0,1:T(8,128)(2,1)S(1)}, bf16[384,512]{0,1:T(8,128)(2,1)}, u32[]{:S(2)}) copy-start(bf16[384,512]{0,1:T(8,128)(2,1)} %copy.108) | copy-start | bytes 1179652
  67.3 8.1 %copy-start.13 = (f32[4,384]{1,0:T(4,128)S(1)}, f32[4,384]{1,0:T(4,128)}, u32[]{:S(2)}) copy-start(f32[4,384]{1,0:T(4,128)} %fusion.16) | copy-start | bytes 18436
  67.3 8.1 %copy-start.15 = (f32[4,384]{1,0:T(4,128)S(1)}, f32[4,384]{1,0:T(4,128)}, u32[]{:S(2)}) copy-start(f32[4,384]{1,0:T(4,128)} %copy-done.14) | copy-start | bytes 18436
  67.3 8.1 %copy-start.7 = (pred[384,384]{0,1:T(8,128)(4,1)S(1)}, pred[384,384]{0,1:T(8,128)(4,1)}, u32[]{:S(2)}) copy-start(pred[384,384]{0,1:T(8,128)(4,1)} %copy-done.6) | copy-start | bytes 442372
  67.3 8.1 %copy-start.10 = (bf16[384,512]{1,0:T(8,128)(2,1)S(1)}, bf16[384,512]{1,0:T(8,128)(2,1)}, u32[]{:S(2)}) copy-start(bf16[384,512]{1,0:T(8,128)(2,1)} %param.16) | copy-start | bytes 1179652
  69.8 179.0 %all-to-all-start.3 = ((bf16[8,2,64,512]{3,2,1,0:T(8,128)(2,1)}), bf16[8,2,64,512]{3,2,1,0:T(8,128)(2,1)}, u32[]{:S(2)}, u32[]{:S(2)}) async-start(bf16[8,2,64,512]{3,2,1,0:T(8,128)(2,1)} %bitcast.118), calls=%async_computation.3 | async-start | bytes 2097152 | tf_op jit(solution)/shard_map/all_to_all | solution.py:143
  74.1 239.4 %reduce-scatter.2.cloned.1.call-start = ((), (), s32[]{:S(2)}) async-start(), calls=%async_computation.5 | async-start | bytes 3932160 | tf_op jit(solution)/shard_map/reduce_scatter | solution.py:186
  77.9 23.5 %collective-permute-start = (bf16[2,384,512]{1,2,0:T(8,128)(2,1)}, bf16[2,384,512]{1,2,0:T(8,128)(2,1)S(1)}, u32[]{:S(2)}, u32[]{:S(2)}) collective-permute-start(bf16[2,384,512]{1,2,0:T(8,128)(2,1)} %get-tuple-element.321), channel_id=1, source_target_pairs={{0,4},{4,8},{8,12},{12,16},{16,20},{20,24},{24,28},{1,5},{5,9},{9,... | collective-permute-start | bytes 2359304 | tf_op jit(solution)/shard_map/while/body/eval_jaxpr/ppermute | solution.py:14
  102.3 27.8 %collective-permute-start = (bf16[2,384,512]{1,2,0:T(8,128)(2,1)}, bf16[2,384,512]{1,2,0:T(8,128)(2,1)S(1)}, u32[]{:S(2)}, u32[]{:S(2)}) collective-permute-start(bf16[2,384,512]{1,2,0:T(8,128)(2,1)} %get-tuple-element.321), channel_id=1, source_target_pairs={{0,4},{4,8},{8,12},{12,16},{16,20},{20,24},{24,28},{1,5},{5,9},{9,... | collective-permute-start | bytes 2359304 | tf_op jit(solution)/shard_map/while/body/eval_jaxpr/ppermute | solution.py:14
  131.0 19.2 %collective-permute-start = (bf16[2,384,512]{1,2,0:T(8,128)(2,1)}, bf16[2,384,512]{1,2,0:T(8,128)(2,1)S(1)}, u32[]{:S(2)}, u32[]{:S(2)}) collective-permute-start(bf16[2,384,512]{1,2,0:T(8,128)(2,1)} %get-tuple-element.321), channel_id=1, source_target_pairs={{0,4},{4,8},{8,12},{12,16},{16,20},{20,24},{24,28},{1,5},{5,9},{9,... | collective-permute-start | bytes 2359304 | tf_op jit(solution)/shard_map/while/body/eval_jaxpr/ppermute | solution.py:14
  151.1 27.8 %collective-permute-start = (bf16[2,384,512]{1,2,0:T(8,128)(2,1)}, bf16[2,384,512]{1,2,0:T(8,128)(2,1)S(1)}, u32[]{:S(2)}, u32[]{:S(2)}) collective-permute-start(bf16[2,384,512]{1,2,0:T(8,128)(2,1)} %get-tuple-element.321), channel_id=1, source_target_pairs={{0,4},{4,8},{8,12},{12,16},{16,20},{20,24},{24,28},{1,5},{5,9},{9,... | collective-permute-start | bytes 2359304 | tf_op jit(solution)/shard_map/while/body/eval_jaxpr/ppermute | solution.py:14
  179.8 19.8 %collective-permute-start = (bf16[2,384,512]{1,2,0:T(8,128)(2,1)}, bf16[2,384,512]{1,2,0:T(8,128)(2,1)S(1)}, u32[]{:S(2)}, u32[]{:S(2)}) collective-permute-start(bf16[2,384,512]{1,2,0:T(8,128)(2,1)} %get-tuple-element.321), channel_id=1, source_target_pairs={{0,4},{4,8},{8,12},{12,16},{16,20},{20,24},{24,28},{1,5},{5,9},{9,... | collective-permute-start | bytes 2359304 | tf_op jit(solution)/shard_map/while/body/eval_jaxpr/ppermute | solution.py:14
  200.4 20.8 %collective-permute-start = (bf16[2,384,512]{1,2,0:T(8,128)(2,1)}, bf16[2,384,512]{1,2,0:T(8,128)(2,1)S(1)}, u32[]{:S(2)}, u32[]{:S(2)}) collective-permute-start(bf16[2,384,512]{1,2,0:T(8,128)(2,1)} %get-tuple-element.321), channel_id=1, source_target_pairs={{0,4},{4,8},{8,12},{12,16},{16,20},{20,24},{24,28},{1,5},{5,9},{9,... | collective-permute-start | bytes 2359304 | tf_op jit(solution)/shard_map/while/body/eval_jaxpr/ppermute | solution.py:14
  222.2 17.9 %collective-permute-start = (bf16[2,384,512]{1,2,0:T(8,128)(2,1)}, bf16[2,384,512]{1,2,0:T(8,128)(2,1)S(1)}, u32[]{:S(2)}, u32[]{:S(2)}) collective-permute-start(bf16[2,384,512]{1,2,0:T(8,128)(2,1)} %get-tuple-element.321), channel_id=1, source_target_pairs={{0,4},{4,8},{8,12},{12,16},{16,20},{20,24},{24,28},{1,5},{5,9},{9,... | collective-permute-start | bytes 2359304 | tf_op jit(solution)/shard_map/while/body/eval_jaxpr/ppermute | solution.py:14
  241.3 7.0 %copy-start.16 = (s32[6,2]{0,1:T(2,128)S(1)}, s32[6,2]{0,1:T(2,128)}, u32[]{:S(2)}) copy-start(s32[6,2]{0,1:T(2,128)} %copy.116) | copy-start | bytes 148
  251.6 5.8 %slice-start = ((s8[6291456]{0:T(1024)(128)(4,1)}), s8[2097152]{0:T(1024)(128)(4,1)S(1)}, s32[]{:S(2)}) async-start(s8[6291456]{0:T(1024)(128)(4,1)} %bitcast.121), calls=%async_computation.6 | async-start | bytes 4194304
  (7 other events, 16.1 us)
Sparse Core Ops, SparseCore 0:
  261.9 51.5 reduce-scatter.1
where the time goes:
time: 321 us; the launch traced here: 320 us
  waiting for transfers between devices  174 us (54%)
  starting transfers between devices  71 us (22%)
  local copies, waits for them, and re-layouts  33.6 us (10%)
  matrix products  22.9 us (7%)
  between operations  13.7 us (4%)
  other arithmetic  4.82 us (2%)
    ppermute x7, waiting for transfers between devices, from_behind(): lax.ppermute(value, axis, [(source, source + steps) for source in range(l...  105 us
    reduce_scatter x1, waiting for transfers between devices, per_device(): lax.psum_scatter(partial_value.astype(jnp.bfloat16), 'mp', scatter_dimens...  51.7 us
    ppermute x7, starting transfers between devices, from_behind(): lax.ppermute(value, axis, [(source, source + steps) for source in range(l...  51.6 us
    all_to_all x1, waiting for transfers between devices, cross_attention(): lax.all_to_all(outgoing, 'seq', split_axis=0, concat_axis=0, tiled=True)  12.4 us
    unnamed x46, local copies, waits for them, and re-layouts  11.9 us
    all_to_all x1, starting transfers between devices, cross_attention(): lax.all_to_all(asked_slots, 'seq', split_axis=0, concat_axis=0, tiled=True)  7.28 us
    dot_general x1, matrix products, per_device(): jnp.dot(attended, out_weight, preferred_element_type=jnp.float32)  6.69 us
  transfers between devices with their start and end apart: 12, of which 11 were waited for; matrix products, arithmetic and copies ran while one was open for 11% of the time, Pallas kernels for 0%

commit v1 on v0

--- a/solution.py
+++ b/solution.py
@@ -6,6 +6,22 @@
 HEAD = 128
 SPAN = 64
 NEG_FILL = -1e30
+
+
+def exchange_in_pairs(shard, axis, split, join):
+    ways, here = (lax.axis_size(axis), lax.axis_index(axis))
+    width = shard.shape[split] // ways
+    dims = list(shard.shape)
+    dims[split] = width
+    height = dims[join]
+    dims[join] = height * ways
+    full = jnp.zeros(dims, shard.dtype)
+    for mask in range(ways):
+        part = lax.dynamic_slice_in_dim(shard, (here ^ mask) * width, width, axis=split)
+        if mask:
+            part = lax.ppermute(part, axis, [(d, d ^ mask) for d in range(ways)])
+        full = lax.dynamic_update_slice_in_dim(full, part, (here ^ mask) * height, axis=join)
+    return full
 
 
 def from_behind(value, axis, steps):
@@ -119,7 +135,7 @@
         devices, capacity
     )
     asked = lax.all_to_all(outgoing, "seq", split_axis=0, concat_axis=0, tiled=True)
-    wanted = lax.all_to_all(asked_slots, "seq", split_axis=0, concat_axis=0, tiled=True)
+    wanted = exchange_in_pairs(asked_slots, "seq", 0, 0)
     source_count = wanted.shape[0]
     item_count = wanted.shape[1]
     key_heads = split_heads(memory_keys[wanted], HEAD)

time: 321 us -> 311 us (0.969)
  waiting for transfers between devices: 174 us -> 154 us
  starting transfers between devices: 71 us -> 82 us
    ppermute x0 -> x7, starting transfers between devices: none -> 13.5 us  [exchange_in_pairs(): part = lax.ppermute(part, axis, [(d, d ^ mask) for d in range(ways)])]
    all_to_all x1, waiting for transfers between devices: 12.4 us -> 0.01 us  [cross_attention(): lax.all_to_all(outgoing, 'seq', split_axis=0, concat_axis=0, tiled=True)]
    ppermute x7, waiting for transfers between devices: 105 us -> 93.7 us  [from_behind(): lax.ppermute(value, axis, [(source, source + steps) for source in range(l...]
    all_to_all x1 -> x0, starting transfers between devices: 7.28 us -> none  [cross_attention(): lax.all_to_all(asked_slots, 'seq', split_axis=0, concat_axis=0, tiled=True)]
    ppermute x0 -> x7, waiting for transfers between devices: none -> 6.82 us  [exchange_in_pairs(): part = lax.ppermute(part, axis, [(d, d ^ mask) for d in range(ways)])]
    unnamed x46 -> x48, local copies, waits for them, and re-layouts: 11.9 us -> 11.3 us
  transfers between devices with their start and end apart: 12 -> 18, of which waited for: 11 -> 14; matrix products, arithmetic and copies ran while one was open for 11% -> 11% of each run, Pallas kernels for 0% -> 0%
where the time goes in v1:
time: 311 us
  waiting for transfers between devices  154 us (50%)
  starting transfers between devices  82 us (26%)
  local copies, waits for them, and re-layouts  32.5 us (10%)
  matrix products  22.9 us (7%)
  between operations  13.8 us (4%)
  other arithmetic  4.82 us (2%)
    ppermute x7, waiting for transfers between devices, from_behind(): lax.ppermute(value, axis, [(source, source + steps) for source in range(l...  93.7 us
    ppermute x7, starting transfers between devices, from_behind(): lax.ppermute(value, axis, [(source, source + steps) for source in range(l...  51.5 us
    reduce_scatter x1, waiting for transfers between devices, per_device(): lax.psum_scatter(partial_value.astype(jnp.bfloat16), 'mp', scatter_dimens...  51.3 us
    ppermute x7, starting transfers between devices, exchange_in_pairs(): part = lax.ppermute(part, axis, [(d, d ^ mask) for d in range(ways)])  13.5 us
    unnamed x48, local copies, waits for them, and re-layouts  11.3 us
    all_to_all x1, starting transfers between devices, cross_attention(): lax.all_to_all(outgoing, 'seq', split_axis=0, concat_axis=0, tiled=True)  7.41 us
    ppermute x7, waiting for transfers between devices, exchange_in_pairs(): part = lax.ppermute(part, axis, [(d, d ^ mask) for d in range(ways)])  6.82 us
    dot_general x1, matrix products, per_device(): jnp.dot(attended, out_weight, preferred_element_type=jnp.float32)  6.67 us
  transfers between devices with their start and end apart: 18, of which 14 were waited for; matrix products, arithmetic and copies ran while one was open for 11% of the time, Pallas kernels for 0%

profile of v1, /device:TPU:0, one launch (start us, length us, event | category | flops | bytes accessed | tf_op | source)
XLA Modules:
  0.0 310.7 jit_solution(15144273376714077580)
XLA Ops:
  11.9 7.4 %all-to-all-start = ((bf16[8,2,64,512]{3,2,1,0:T(8,128)(2,1)}), bf16[8,2,64,512]{3,2,1,0:T(8,128)(2,1)}, u32[]{:S(2)}, u32[]{:S(2)}) async-start(bf16[8,2,64,512]{3,2,1,0:T(8,128)(2,1)} %bitcast.37), calls=%async_computation | async-start | bytes 2097152 | tf_op jit(solution)/shard_map/all_to_all | solution.py:137
  19.7 4.8 %collective-permute-start.7 = (s32[1,2]{1,0:T(1,128)S(1)}, s32[1,2]{1,0:T(1,128)S(1)}, u32[]{:S(2)}, u32[]{:S(2)}) collective-permute-start(s32[1,2]{1,0:T(1,128)S(1)} %get-tuple-element.248), channel_id=1, source_target_pairs={{0,28},{4,24},{8,20},{12,16},{16,12},{20,8},{24,4},{28,0},{1,29},{... | collective-permute-start | bytes 32 | tf_op jit(solution)/shard_map/ppermute | solution.py:22
  52.9 3.6 %multiply_reduce_fusion.2 = (f32[8,2,4,64]{3,2,1,0:T(4,128)S(1)}, f32[8,2,4,64,128]{4,3,2,1,0:T(8,128)S(1)}) fusion(bf16[8,2,128,4,128]{4,3,2,1,0:T(4,128)(2,1)} %reshape.124, bf16[8,2,64,512]{3,2,1,0:T(8,128)(2,1)} %all-to-all-done), kind=kOutput, calls=%fused_computation.28 | convolution fusion | flops 135262208 | bytes 5259264 | tf_op jit(solution)/shard_map/nicha,nikha->nihck/dot_general | solution.py:144
  60.5 5.1 %all-to-all-start.1 = ((bf16[8,2,256]{2,1,0:T(2,128)(2,1)}), bf16[8,2,256]{2,1,0:T(2,128)(2,1)S(1)}, u32[]{:S(2)}, u32[]{:S(2)}) async-start(bf16[8,2,256]{2,1,0:T(2,128)(2,1)} %reshape.154), calls=%async_computation.1 | async-start | bytes 16384 | tf_op jit(solution)/shard_map/all_to_all | solution.py:160
  72.1 4.2 %all-to-all-start.2 = ((bf16[8,2,64,512]{3,2,1,0:T(8,128)(2,1)}), bf16[8,2,64,512]{3,2,1,0:T(8,128)(2,1)}, u32[]{:S(2)}, u32[]{:S(2)}) async-start(bf16[8,2,64,512]{3,2,1,0:T(8,128)(2,1)} %bitcast.113), calls=%async_computation.2 | async-start | bytes 2097152 | tf_op jit(solution)/shard_map/all_to_all | solution.py:159
  80.1 151.6 %while.21 = (s32[]{:T(128)}, bf16[2,384,512]{1,2,0:T(8,128)(2,1)}, f32[4,384]{1,0:T(4,128)S(1)}, f32[4,384]{1,0:T(4,128)S(1)}, f32[4,384,128]{2,1,0:T(8,128)S(1)...) while((s32[]{:T(128)}, bf16[2,384,512]{1,2,0:T(8,128)(2,1)}, ...), condition=%wide.region_7.8_spmd, body=%wide.region_2.7_spmd.sunk | while | flops 307104768 | bytes 16220540 | solution.py:100
  80.2 3.6 %collective-permute-start = (bf16[2,384,512]{1,2,0:T(8,128)(2,1)}, bf16[2,384,512]{1,2,0:T(8,128)(2,1)S(1)}, u32[]{:S(2)}, u32[]{:S(2)}) collective-permute-start(bf16[2,384,512]{1,2,0:T(8,128)(2,1)} %get-tuple-element.329), channel_id=1, source_target_pairs={{0,4},{4,8},{8,12},{12,16},{16,20},{20,24},{24,28},{1,5},{5,9},{9,... | collective-permute-start | bytes 2359304 | tf_op jit(solution)/shard_map/while/body/eval_jaxpr/ppermute | solution.py:30
  83.8 19.2 %collective-permute-done = bf16[2,384,512]{1,2,0:T(8,128)(2,1)S(1)} collective-permute-done((bf16[2,384,512]{1,2,0:T(8,128)(2,1)}, bf16[2,384,512]{1,2,0:T(8,128)(2,1)S(1)}, u32[]{:S(2)}, u32[]{:S(2)}) %collective-permute-start) | collective-permute-done | bytes 786464 | tf_op jit(solution)/shard_map/while/body/eval_jaxpr/ppermute | solution.py:30
  103.9 10.5 %collective-permute-start = (bf16[2,384,512]{1,2,0:T(8,128)(2,1)}, bf16[2,384,512]{1,2,0:T(8,128)(2,1)S(1)}, u32[]{:S(2)}, u32[]{:S(2)}) collective-permute-start(bf16[2,384,512]{1,2,0:T(8,128)(2,1)} %get-tuple-element.329), channel_id=1, source_target_pairs={{0,4},{4,8},{8,12},{12,16},{16,20},{20,24},{24,28},{1,5},{5,9},{9,... | collective-permute-start | bytes 2359304 | tf_op jit(solution)/shard_map/while/body/eval_jaxpr/ppermute | solution.py:30
  114.4 12.7 %collective-permute-done = bf16[2,384,512]{1,2,0:T(8,128)(2,1)S(1)} collective-permute-done((bf16[2,384,512]{1,2,0:T(8,128)(2,1)}, bf16[2,384,512]{1,2,0:T(8,128)(2,1)S(1)}, u32[]{:S(2)}, u32[]{:S(2)}) %collective-permute-start) | collective-permute-done | bytes 786464 | tf_op jit(solution)/shard_map/while/body/eval_jaxpr/ppermute | solution.py:30
  128.0 5.2 %collective-permute-start = (bf16[2,384,512]{1,2,0:T(8,128)(2,1)}, bf16[2,384,512]{1,2,0:T(8,128)(2,1)S(1)}, u32[]{:S(2)}, u32[]{:S(2)}) collective-permute-start(bf16[2,384,512]{1,2,0:T(8,128)(2,1)} %get-tuple-element.329), channel_id=1, source_target_pairs={{0,4},{4,8},{8,12},{12,16},{16,20},{20,24},{24,28},{1,5},{5,9},{9,... | collective-permute-start | bytes 2359304 | tf_op jit(solution)/shard_map/while/body/eval_jaxpr/ppermute | solution.py:30
  133.3 11.8 %collective-permute-done = bf16[2,384,512]{1,2,0:T(8,128)(2,1)S(1)} collective-permute-done((bf16[2,384,512]{1,2,0:T(8,128)(2,1)}, bf16[2,384,512]{1,2,0:T(8,128)(2,1)S(1)}, u32[]{:S(2)}, u32[]{:S(2)}) %collective-permute-start) | collective-permute-done | bytes 786464 | tf_op jit(solution)/shard_map/while/body/eval_jaxpr/ppermute | solution.py:30
  145.9 14.5 %collective-permute-start = (bf16[2,384,512]{1,2,0:T(8,128)(2,1)}, bf16[2,384,512]{1,2,0:T(8,128)(2,1)S(1)}, u32[]{:S(2)}, u32[]{:S(2)}) collective-permute-start(bf16[2,384,512]{1,2,0:T(8,128)(2,1)} %get-tuple-element.329), channel_id=1, source_target_pairs={{0,4},{4,8},{8,12},{12,16},{16,20},{20,24},{24,28},{1,5},{5,9},{9,... | collective-permute-start | bytes 2359304 | tf_op jit(solution)/shard_map/while/body/eval_jaxpr/ppermute | solution.py:30
  160.4 13.9 %collective-permute-done = bf16[2,384,512]{1,2,0:T(8,128)(2,1)S(1)} collective-permute-done((bf16[2,384,512]{1,2,0:T(8,128)(2,1)}, bf16[2,384,512]{1,2,0:T(8,128)(2,1)S(1)}, u32[]{:S(2)}, u32[]{:S(2)}) %collective-permute-start) | collective-permute-done | bytes 786464 | tf_op jit(solution)/shard_map/while/body/eval_jaxpr/ppermute | solution.py:30
  175.2 5.2 %collective-permute-start = (bf16[2,384,512]{1,2,0:T(8,128)(2,1)}, bf16[2,384,512]{1,2,0:T(8,128)(2,1)S(1)}, u32[]{:S(2)}, u32[]{:S(2)}) collective-permute-start(bf16[2,384,512]{1,2,0:T(8,128)(2,1)} %get-tuple-element.329), channel_id=1, source_target_pairs={{0,4},{4,8},{8,12},{12,16},{16,20},{20,24},{24,28},{1,5},{5,9},{9,... | collective-permute-start | bytes 2359304 | tf_op jit(solution)/shard_map/while/body/eval_jaxpr/ppermute | solution.py:30
  180.5 13.0 %collective-permute-done = bf16[2,384,512]{1,2,0:T(8,128)(2,1)S(1)} collective-permute-done((bf16[2,384,512]{1,2,0:T(8,128)(2,1)}, bf16[2,384,512]{1,2,0:T(8,128)(2,1)S(1)}, u32[]{:S(2)}, u32[]{:S(2)}) %collective-permute-start) | collective-permute-done | bytes 786464 | tf_op jit(solution)/shard_map/while/body/eval_jaxpr/ppermute | solution.py:30
  194.3 7.2 %collective-permute-start = (bf16[2,384,512]{1,2,0:T(8,128)(2,1)}, bf16[2,384,512]{1,2,0:T(8,128)(2,1)S(1)}, u32[]{:S(2)}, u32[]{:S(2)}) collective-permute-start(bf16[2,384,512]{1,2,0:T(8,128)(2,1)} %get-tuple-element.329), channel_id=1, source_target_pairs={{0,4},{4,8},{8,12},{12,16},{16,20},{20,24},{24,28},{1,5},{5,9},{9,... | collective-permute-start | bytes 2359304 | tf_op jit(solution)/shard_map/while/body/eval_jaxpr/ppermute | solution.py:30
  201.5 12.0 %collective-permute-done = bf16[2,384,512]{1,2,0:T(8,128)(2,1)S(1)} collective-permute-done((bf16[2,384,512]{1,2,0:T(8,128)(2,1)}, bf16[2,384,512]{1,2,0:T(8,128)(2,1)S(1)}, u32[]{:S(2)}, u32[]{:S(2)}) %collective-permute-start) | collective-permute-done | bytes 786464 | tf_op jit(solution)/shard_map/while/body/eval_jaxpr/ppermute | solution.py:30
  214.5 5.2 %collective-permute-start = (bf16[2,384,512]{1,2,0:T(8,128)(2,1)}, bf16[2,384,512]{1,2,0:T(8,128)(2,1)S(1)}, u32[]{:S(2)}, u32[]{:S(2)}) collective-permute-start(bf16[2,384,512]{1,2,0:T(8,128)(2,1)} %get-tuple-element.329), channel_id=1, source_target_pairs={{0,4},{4,8},{8,12},{12,16},{16,20},{20,24},{24,28},{1,5},{5,9},{9,... | collective-permute-start | bytes 2359304 | tf_op jit(solution)/shard_map/while/body/eval_jaxpr/ppermute | solution.py:30
  219.7 11.1 %collective-permute-done = bf16[2,384,512]{1,2,0:T(8,128)(2,1)S(1)} collective-permute-done((bf16[2,384,512]{1,2,0:T(8,128)(2,1)}, bf16[2,384,512]{1,2,0:T(8,128)(2,1)S(1)}, u32[]{:S(2)}, u32[]{:S(2)}) %collective-permute-start) | collective-permute-done | bytes 786464 | tf_op jit(solution)/shard_map/while/body/eval_jaxpr/ppermute | solution.py:30
  232.1 6.7 %fusion.65 = f32[384,4096]{1,0:T(8,128)} fusion(bf16[384,512]{0,1:T(8,128)(2,1)S(1)} %bitcast.123, bf16[512,4096]{1,0:T(8,128)(2,1)} %param.22), kind=kOutput, calls=%fused_computation.97 | convolution fusion | flops 1610612736 | bytes 10878976 | tf_op jit(solution)/shard_map/dot_general | solution.py:198
  239.6 2.8 copy.130
  248.9 3.6 %add_convert_fusion = bf16[384,4096]{1,0:T(8,128)(2,1)} fusion(f32[384,4096]{1,0:T(8,128)S(1)} %bitcast.117, bf16[512,4096]{1,0:T(8,128)(2,1)S(1)} %copy-done.2, bf16[48,8,4,128]{3,2,1,0:T(4,128)(2,1)S(1)} %bitcast.120), kind=kOutput, calls=%fused_computation.16 | convolution fusion | flops 1613758464 | bytes 14024704 | tf_op jit(solution)/shard_map/dot_general | solution.py:199
  252.5 51.3 %reduce-scatter.2.cloned.1.call-done = bf16[384,1024]{1,0:T(8,128)(2,1)} async-done(((bf16[384,4096]{1,0:T(8,128)(2,1)}), bf16[384,1024]{1,0:T(8,128)(2,1)}) %reduce-scatter.2.cloned.1.call-update) | async-done | bytes 786448 | tf_op jit(solution)/shard_map/reduce_scatter | solution.py:202
  (135 shorter events, 62.0 us)
Async XLA Ops:
  6.5 39.6 %copy-start = (bf16[8,128,512]{2,1,0:T(8,128)(2,1)S(1)}, bf16[8,128,512]{2,1,0:T(8,128)(2,1)}, u32[]{:S(2)}) copy-start(bf16[8,128,512]{2,1,0:T(8,128)(2,1)} %param.19) | copy-start | bytes 3145732
  10.4 8.9 %copy-start.17 = (s32[6,2]{0,1:T(2,128)S(1)}, s32[6,2]{0,1:T(2,128)}, u32[]{:S(2)}) copy-start(s32[6,2]{0,1:T(2,128)} %param.21) | copy-start | bytes 148
  10.5 17.8 %copy-start.8 = (bf16[384,512]{1,0:T(8,128)(2,1)S(1)}, bf16[384,512]{1,0:T(8,128)(2,1)}, u32[]{:S(2)}) copy-start(bf16[384,512]{1,0:T(8,128)(2,1)} %param.15) | copy-start | bytes 1179652
  10.5 18.7 %copy-start.9 = (bf16[384,512]{1,0:T(8,128)(2,1)S(1)}, bf16[384,512]{1,0:T(8,128)(2,1)}, u32[]{:S(2)}) copy-start(bf16[384,512]{1,0:T(8,128)(2,1)} %param.16) | copy-start | bytes 1179652
  11.9 18.3 %copy-start.1 = (bf16[384,512]{1,0:T(8,128)(2,1)S(1)}, bf16[384,512]{1,0:T(8,128)(2,1)}, u32[]{:S(2)}) copy-start(bf16[384,512]{1,0:T(8,128)(2,1)} %param.14) | copy-start | bytes 1179652
  11.9 41.0 %all-to-all-start = ((bf16[8,2,64,512]{3,2,1,0:T(8,128)(2,1)}), bf16[8,2,64,512]{3,2,1,0:T(8,128)(2,1)}, u32[]{:S(2)}, u32[]{:S(2)}) async-start(bf16[8,2,64,512]{3,2,1,0:T(8,128)(2,1)} %bitcast.37), calls=%async_computation | async-start | bytes 2097152 | tf_op jit(solution)/shard_map/all_to_all | solution.py:137
  19.7 26.4 %collective-permute-start.7 = (s32[1,2]{1,0:T(1,128)S(1)}, s32[1,2]{1,0:T(1,128)S(1)}, u32[]{:S(2)}, u32[]{:S(2)}) collective-permute-start(s32[1,2]{1,0:T(1,128)S(1)} %get-tuple-element.248), channel_id=1, source_target_pairs={{0,28},{4,24},{8,20},{12,16},{16,12},{20,8},{24,4},{28,0},{1,29},{... | collective-permute-start | bytes 32 | tf_op jit(solution)/shard_map/ppermute | solution.py:22
  24.5 21.5 %collective-permute-start.6 = (s32[1,2]{1,0:T(1,128)S(1)}, s32[1,2]{1,0:T(1,128)S(1)}, u32[]{:S(2)}, u32[]{:S(2)}) collective-permute-start(s32[1,2]{1,0:T(1,128)S(1)} %get-tuple-element.249), channel_id=1, source_target_pairs={{0,24},{4,28},{8,16},{12,20},{16,8},{20,12},{24,0},{28,4},{1,25},{... | collective-permute-start | bytes 32 | tf_op jit(solution)/shard_map/ppermute | solution.py:22
  25.0 21.0 %collective-permute-start.5 = (s32[1,2]{1,0:T(1,128)S(1)}, s32[1,2]{1,0:T(1,128)S(1)}, u32[]{:S(2)}, u32[]{:S(2)}) collective-permute-start(s32[1,2]{1,0:T(1,128)S(1)} %get-tuple-element.250), channel_id=1, source_target_pairs={{0,20},{4,16},{8,28},{12,24},{16,4},{20,0},{24,12},{28,8},{1,21},{... | collective-permute-start | bytes 32 | tf_op jit(solution)/shard_map/ppermute | solution.py:22
  25.6 19.6 %collective-permute-start.4 = (s32[1,2]{1,0:T(1,128)S(1)}, s32[1,2]{1,0:T(1,128)S(1)}, u32[]{:S(2)}, u32[]{:S(2)}) collective-permute-start(s32[1,2]{1,0:T(1,128)S(1)} %get-tuple-element.251), channel_id=1, source_target_pairs={{0,16},{4,20},{8,24},{12,28},{16,0},{20,4},{24,8},{28,12},{1,17},{... | collective-permute-start | bytes 32 | tf_op jit(solution)/shard_map/ppermute | solution.py:22
  30.8 15.4 %copy-start.14 = (f32[4,384]{1,0:T(4,128)}, f32[4,384]{1,0:T(4,128)S(1)}, u32[]{:S(2)}) copy-start(f32[4,384]{1,0:T(4,128)S(1)} %get-tuple-element.256) | copy-start | bytes 18436
  33.3 3.5 %collective-permute-start.1 = (s32[1,2]{1,0:T(1,128)S(1)}, s32[1,2]{1,0:T(1,128)S(1)}, u32[]{:S(2)}, u32[]{:S(2)}) collective-permute-start(s32[1,2]{1,0:T(1,128)S(1)} %get-tuple-element.254), channel_id=1, source_target_pairs={{0,4},{4,0},{8,12},{12,8},{16,20},{20,16},{24,28},{28,24},{1,5},{5... | collective-permute-start | bytes 32 | tf_op jit(solution)/shard_map/ppermute | solution.py:22
  36.9 3.6 %collective-permute-start.2 = (s32[1,2]{1,0:T(1,128)S(1)}, s32[1,2]{1,0:T(1,128)S(1)}, u32[]{:S(2)}, u32[]{:S(2)}) collective-permute-start(s32[1,2]{1,0:T(1,128)S(1)} %get-tuple-element.253), channel_id=1, source_target_pairs={{0,8},{4,12},{8,0},{12,4},{16,24},{20,28},{24,16},{28,20},{1,9},{5... | collective-permute-start | bytes 32 | tf_op jit(solution)/shard_map/ppermute | solution.py:22
  40.5 4.6 %collective-permute-start.3 = (s32[1,2]{1,0:T(1,128)S(1)}, s32[1,2]{1,0:T(1,128)S(1)}, u32[]{:S(2)}, u32[]{:S(2)}) collective-permute-start(s32[1,2]{1,0:T(1,128)S(1)} %get-tuple-element.252), channel_id=1, source_target_pairs={{0,12},{4,8},{8,4},{12,0},{16,28},{20,24},{24,20},{28,16},{1,13},{... | collective-permute-start | bytes 32 | tf_op jit(solution)/shard_map/ppermute | solution.py:22
  60.5 11.6 %all-to-all-start.1 = ((bf16[8,2,256]{2,1,0:T(2,128)(2,1)}), bf16[8,2,256]{2,1,0:T(2,128)(2,1)S(1)}, u32[]{:S(2)}, u32[]{:S(2)}) async-start(bf16[8,2,256]{2,1,0:T(2,128)(2,1)} %reshape.154), calls=%async_computation.1 | async-start | bytes 16384 | tf_op jit(solution)/shard_map/all_to_all | solution.py:160
  72.1 167.5 %all-to-all-start.2 = ((bf16[8,2,64,512]{3,2,1,0:T(8,128)(2,1)}), bf16[8,2,64,512]{3,2,1,0:T(8,128)(2,1)}, u32[]{:S(2)}, u32[]{:S(2)}) async-start(bf16[8,2,64,512]{3,2,1,0:T(8,128)(2,1)} %bitcast.113), calls=%async_computation.2 | async-start | bytes 2097152 | tf_op jit(solution)/shard_map/all_to_all | solution.py:159
  76.3 227.5 %reduce-scatter.2.cloned.1.call-start = ((), (), s32[]{:S(2)}) async-start(), calls=%async_computation.4 | async-start | bytes 3932160 | tf_op jit(solution)/shard_map/reduce_scatter | solution.py:202
  80.2 22.8 %collective-permute-start = (bf16[2,384,512]{1,2,0:T(8,128)(2,1)}, bf16[2,384,512]{1,2,0:T(8,128)(2,1)S(1)}, u32[]{:S(2)}, u32[]{:S(2)}) collective-permute-start(bf16[2,384,512]{1,2,0:T(8,128)(2,1)} %get-tuple-element.329), channel_id=1, source_target_pairs={{0,4},{4,8},{8,12},{12,16},{16,20},{20,24},{24,28},{1,5},{5,9},{9,... | collective-permute-start | bytes 2359304 | tf_op jit(solution)/shard_map/while/body/eval_jaxpr/ppermute | solution.py:30
  103.9 23.3 %collective-permute-start = (bf16[2,384,512]{1,2,0:T(8,128)(2,1)}, bf16[2,384,512]{1,2,0:T(8,128)(2,1)S(1)}, u32[]{:S(2)}, u32[]{:S(2)}) collective-permute-start(bf16[2,384,512]{1,2,0:T(8,128)(2,1)} %get-tuple-element.329), channel_id=1, source_target_pairs={{0,4},{4,8},{8,12},{12,16},{16,20},{20,24},{24,28},{1,5},{5,9},{9,... | collective-permute-start | bytes 2359304 | tf_op jit(solution)/shard_map/while/body/eval_jaxpr/ppermute | solution.py:30
  128.0 17.0 %collective-permute-start = (bf16[2,384,512]{1,2,0:T(8,128)(2,1)}, bf16[2,384,512]{1,2,0:T(8,128)(2,1)S(1)}, u32[]{:S(2)}, u32[]{:S(2)}) collective-permute-start(bf16[2,384,512]{1,2,0:T(8,128)(2,1)} %get-tuple-element.329), channel_id=1, source_target_pairs={{0,4},{4,8},{8,12},{12,16},{16,20},{20,24},{24,28},{1,5},{5,9},{9,... | collective-permute-start | bytes 2359304 | tf_op jit(solution)/shard_map/while/body/eval_jaxpr/ppermute | solution.py:30
  145.9 28.4 %collective-permute-start = (bf16[2,384,512]{1,2,0:T(8,128)(2,1)}, bf16[2,384,512]{1,2,0:T(8,128)(2,1)S(1)}, u32[]{:S(2)}, u32[]{:S(2)}) collective-permute-start(bf16[2,384,512]{1,2,0:T(8,128)(2,1)} %get-tuple-element.329), channel_id=1, source_target_pairs={{0,4},{4,8},{8,12},{12,16},{16,20},{20,24},{24,28},{1,5},{5,9},{9,... | collective-permute-start | bytes 2359304 | tf_op jit(solution)/shard_map/while/body/eval_jaxpr/ppermute | solution.py:30
  175.2 18.2 %collective-permute-start = (bf16[2,384,512]{1,2,0:T(8,128)(2,1)}, bf16[2,384,512]{1,2,0:T(8,128)(2,1)S(1)}, u32[]{:S(2)}, u32[]{:S(2)}) collective-permute-start(bf16[2,384,512]{1,2,0:T(8,128)(2,1)} %get-tuple-element.329), channel_id=1, source_target_pairs={{0,4},{4,8},{8,12},{12,16},{16,20},{20,24},{24,28},{1,5},{5,9},{9,... | collective-permute-start | bytes 2359304 | tf_op jit(solution)/shard_map/while/body/eval_jaxpr/ppermute | solution.py:30
  194.3 19.3 %collective-permute-start = (bf16[2,384,512]{1,2,0:T(8,128)(2,1)}, bf16[2,384,512]{1,2,0:T(8,128)(2,1)S(1)}, u32[]{:S(2)}, u32[]{:S(2)}) collective-permute-start(bf16[2,384,512]{1,2,0:T(8,128)(2,1)} %get-tuple-element.329), channel_id=1, source_target_pairs={{0,4},{4,8},{8,12},{12,16},{16,20},{20,24},{24,28},{1,5},{5,9},{9,... | collective-permute-start | bytes 2359304 | tf_op jit(solution)/shard_map/while/body/eval_jaxpr/ppermute | solution.py:30
  214.5 16.4 %collective-permute-start = (bf16[2,384,512]{1,2,0:T(8,128)(2,1)}, bf16[2,384,512]{1,2,0:T(8,128)(2,1)S(1)}, u32[]{:S(2)}, u32[]{:S(2)}) collective-permute-start(bf16[2,384,512]{1,2,0:T(8,128)(2,1)} %get-tuple-element.329), channel_id=1, source_target_pairs={{0,4},{4,8},{8,12},{12,16},{16,20},{20,24},{24,28},{1,5},{5,9},{9,... | collective-permute-start | bytes 2359304 | tf_op jit(solution)/shard_map/while/body/eval_jaxpr/ppermute | solution.py:30
  (14 other events, 74.8 us)
Sparse Core Ops, SparseCore 0:
  252.6 51.1 reduce-scatter.1
